TPU v7x, 32 devices: a whole 2x2x4 slice. The times are simulated.
32 devices in a mesh: src: 4 (over x, core), rcv: 8 (over z, y).
Axes of the slice: x: 2, y: 2, z: 4, core: 2. Of those that a mesh axis runs over, the one named last changes fastest.
Arguments:
- spectra: bfloat16 [2, 8, 192, 2048], P(None, None, 'src', 'rcv'), as said below
- alive: int32 [192, 2048], P('src', 'rcv'), may hold values 0 or 1
Outputs:
- stacked: bfloat16 [2, 8, 2048, 2048], P(None, None, 'src', 'rcv')
Inputs may be any that keep to these rules, and one draw needn't show every extreme that they name: spectra: every entry is a random factor times an amplitude of its window and channel that spreads over a factor of 15.
All inputs are finite; a program needn't handle non-finite values. No bound on the sum of `alive` on one device may be relied on, other than what follows from the above.
Results may differ from a plain program's by a relative error of at most 0.0057.
Values may be sent and summed in bfloat16 or wider, within the bound.
A program may use at most 64 MiB of HBM per device.

v0:
```python
import jax
import jax.numpy as jnp
from jax import lax
from jax.sharding import PartitionSpec as P


def spread(block, axis, holder):
    block = jnp.where(lax.axis_index(axis) == holder, block, jnp.zeros_like(block))
    return lax.psum(block, axis)


def whiten(spectra, alive, bins):
    values = spectra.astype(jnp.float32)
    power = jnp.sum(values * values, axis=(0, 1)) / bins
    factor = alive.astype(jnp.float32) / jnp.sqrt(jnp.maximum(power, 0.5))
    return (values * factor).astype(jnp.bfloat16)


def cross_terms(source_part, receiver_part):
    swapped = jnp.stack((receiver_part[1], -receiver_part[0]))
    real_sum = jnp.einsum(
        "kfwc,kfwd->fcd", source_part, receiver_part, preferred_element_type=jnp.float32
    )
    imag_sum = jnp.einsum(
        "kfwc,kfwd->fcd", source_part, swapped, preferred_element_type=jnp.float32
    )
    return jnp.stack((real_sum, imag_sum))


def body(spectra, alive):
    bins = spectra.shape[1]
    whitened = whiten(spectra, alive, bins)
    ratio = lax.axis_size("rcv") // lax.axis_size("src")
    row_index = lax.axis_index("src")
    receivers = lax.all_gather(whitened, "src", axis=2, tiled=True)
    blocks = []
    for offset in range(ratio):
        blocks.append(spread(receivers, "rcv", row_index * ratio + offset))
    sources = jnp.concatenate(blocks, axis=3)
    stacked = cross_terms(sources, receivers)
    total_windows = receivers.shape[2]
    factor = jnp.float32(1.0) / jnp.sqrt(jnp.float32(total_windows))
    return (stacked * factor).astype(jnp.bfloat16)


def solution(mesh):
    return jax.shard_map(
        body,
        mesh=mesh,
        in_specs=(P(None, None, "src", "rcv"), P("src", "rcv")),
        out_specs=P(None, None, "src", "rcv"),
        check_vma=False,
    )
```

profile of v0, /device:TPU:3, one launch (start us, length us, event | category | flops | bytes accessed | tf_op | source)
XLA Modules:
  0.0 178.7 jit_solution(7315935909044241583)
XLA Ops:
  6.5 0.0 all-gather.2.cloned.1.call-start
  6.5 1.1 fusion.4
  7.6 0.8 rsqrt_multiply_fusion
  8.4 1.8 %fusion.5 = bf16[2,8,48,256]{3,2,0,1:T(8,128)(2,1)} fusion(f32[48,256]{1,0:T(8,128)S(1)} %rsqrt_multiply_fusion, bf16[2,8,48,256]{3,2,1,0:T(8,128)(2,1)} %param.2), kind=kLoop, calls=%fused_computation.12 | loop fusion | flops 589824 | bytes 835584 | tf_op jit(solution)/shard_map/convert_element_type | solution.py:16
  10.3 0.0 all-gather.2.cloned.1.call-update
  10.3 0.0 all-reduce.3.cloned.1.call-start
  10.3 20.2 %all-gather.2.cloned.1.call-done = bf16[2,8,192,256]{3,2,0,1:T(8,128)(2,1)} async-done(((bf16[2,8,48,256]{3,2,0,1:T(8,128)(2,1)}), bf16[2,8,192,256]{3,2,0,1:T(8,128)(2,1)}) %all-gather.2.cloned.1.call-update) | async-done | bytes 1572880 | tf_op jit(solution)/shard_map/all_gather | solution.py:35
  30.6 0.0 copy-start
  30.6 3.4 %broadcast_select_fusion = (bf16[2,8,192,256]{3,2,0,1:T(8,128)(2,1)}, bf16[2,8,192,256]{3,2,0,1:T(8,128)(2,1)}) fusion(bf16[2,8,192,256]{3,2,0,1:T(8,128)(2,1)} %all-gather.2.cloned.1.call-done, pred[]{:T(512)S(6)} %eq.7, pred[]{:T(512)S(6)} %eq.6), kind=kLoop, calls=%fused_computation.7 | loop fusion | flops 1572864 | bytes 4718594 | tf_op jit(solution)/shard_map/jit(_where)/select_n | solution.py:8
  34.0 0.0 all-reduce.3.cloned.1.call-update
  34.0 0.0 copy-done
  34.0 0.1 fusion.7
  34.1 130.3 %all-reduce.3.cloned.1.call-done = (bf16[2,8,192,256]{3,2,0,1:T(8,128)(2,1)}, bf16[2,8,192,256]{3,2,0,1:T(8,128)(2,1)}) async-done(((bf16[2,8,192,256]{3,2,0,1:T(8,128)(2,1)}, bf16[2,8,192,256]{3,2,0,1:T(8,128)(2,1)}), (bf16[2,8,192,256]{3,2,0,1:T(8,128)(2,1)}, bf16[2,8,192,256]{3,2,0,1:T(8,128)(2,1)})) %all-reduce.3.cloned.1.call-update) | async-done | bytes 3145744 | tf_op jit(solution)/shard_map/psum | solution.py:9
  164.4 0.0 copy-start.1
  164.4 1.7 constant_dynamic-update-slice_fusion.1
  166.1 0.2 copy-done.1
  166.3 0.1 constant_dynamic-update-slice_fusion
  166.4 1.4 convolution_bitcast_fusion
  167.9 1.4 convolution_bitcast_fusion.1
  169.3 2.6 %fusion = bf16[2,8,512,256]{3,2,1,0:T(8,128)(2,1)} fusion(f32[1,8,512,256]{3,2,1,0:T(8,128)S(1)} %convolution_bitcast_fusion, f32[1,8,512,256]{3,2,1,0:T(8,128)S(1)} %convolution_bitcast_fusion.1), kind=kLoop, calls=%fused_computation.1 | loop fusion | flops 6291456 | bytes 12582912 | tf_op jit(solution)/shard_map/convert_element_type | solution.py:43
Async XLA Ops:
  6.5 24.0 %all-gather.2.cloned.1.call-start = ((), (), s32[]{:S(2)}) async-start(), calls=%async_computation | async-start | bytes 1966080 | tf_op jit(solution)/shard_map/all_gather | solution.py:35
  10.3 154.1 %all-reduce.3.cloned.1.call-start = ((), (), s32[]{:S(2)}) async-start(), calls=%async_computation.1 | async-start | bytes 6291456 | tf_op jit(solution)/shard_map/psum | solution.py:9
  30.6 3.4 %copy-start = (bf16[2,8,192,256]{3,2,0,1:T(8,128)(2,1)S(1)}, bf16[2,8,192,256]{3,2,0,1:T(8,128)(2,1)}, u32[]{:S(2)}) copy-start(bf16[2,8,192,256]{3,2,0,1:T(8,128)(2,1)} %all-gather.2.cloned.1.call-done) | copy-start | bytes 4718596
  164.4 1.9 %copy-start.1 = (bf16[2,8,192,256]{3,2,0,1:T(8,128)(2,1)S(1)}, bf16[2,8,192,256]{3,2,0,1:T(8,128)(2,1)}, u32[]{:S(2)}) copy-start(bf16[2,8,192,256]{3,2,0,1:T(8,128)(2,1)} %get-tuple-element.6) | copy-start | bytes 4718596
Sparse Core Ops, SparseCore 0:
  10.4 20.1 all-gather.1
  34.2 130.1 all-reduce.2
where the time goes:
time: 180 us; the launch traced here: 179 us
  waiting for transfers between devices  151 us (84%)
  between operations  13.5 us (8%)
  other arithmetic  9.79 us (5%)
  matrix products  2.88 us (2%)
  local copies, waits for them, and re-layouts  2.01 us (1%)
    psum x1, waiting for transfers between devices, spread(): return lax.psum(block, axis)  130 us
    all_gather x1, waiting for transfers between devices, body(): receivers = lax.all_gather(whitened, 'src', axis=2, tiled=True)  20.2 us
  transfers between devices with their start and end apart: 2, of which 2 were waited for; matrix products, arithmetic and copies ran while one was open for 0% of the time, Pallas kernels for 0%

commit v1 on v0

--- a/solution.py
+++ b/solution.py
@@ -1,7 +1,16 @@
+import functools
+
 import jax
 import jax.numpy as jnp
 from jax import lax
+from jax.experimental import pallas as pl
+from jax.experimental.pallas import tpu as pltpu
 from jax.sharding import PartitionSpec as P
+
+MESH = pl.DeviceIdType.MESH
+
+N_VIA_X = 0
+N_Y_ONCE = 0
 
 
 def spread(block, axis, holder):
@@ -27,7 +36,7 @@
     return jnp.stack((real_sum, imag_sum))
 
 
-def body(spectra, alive):
+def general_body(spectra, alive):
     bins = spectra.shape[1]
     whitened = whiten(spectra, alive, bins)
     ratio = lax.axis_size("rcv") // lax.axis_size("src")
@@ -43,7 +52,222 @@
     return (stacked * factor).astype(jnp.bfloat16)
 
 
+def kernel(
+    n_z,
+    spectra_ref,
+    alive_ref,
+    out_ref,
+    col,
+    srcs,
+    rhs,
+    stage,
+    r_sib,
+    r_x,
+    r_fwd,
+    r_own,
+    r_oth,
+    s_sib,
+    s_x,
+    s_fwd,
+    s_up,
+    s_dn,
+    s_y,
+    o_sem,
+):
+    bins, windows, channels = spectra_ref.shape[1:]
+    s = lax.axis_index("src")
+    r = lax.axis_index("rcv")
+    y = lax.rem(r, 2)
+    z = r // 2
+    sib = s + 1 - 2 * lax.rem(s, 2)
+    xp = lax.rem(s + 2, 4)
+    diag = lax.rem(sib + 2, 4)
+    ry = r + 1 - 2 * y
+    oy = 1 - y
+    is_root = z == s
+    up_ok = jnp.logical_and(z >= s, z < n_z - 1)
+    dn_ok = jnp.logical_and(z <= s, z > 0)
+
+    barrier = pltpu.get_barrier_semaphore()
+    for target in ((sib, r), (xp, r), (s, ry)):
+        pl.semaphore_signal(barrier, inc=1, device_id=target, device_id_type=MESH)
+
+    @pl.when(z < n_z - 1)
+    def _():
+        pl.semaphore_signal(barrier, inc=1, device_id=(s, r + 2), device_id_type=MESH)
+
+    @pl.when(z > 0)
+    def _():
+        pl.semaphore_signal(barrier, inc=1, device_id=(s, r - 2), device_id_type=MESH)
+
+    power = jnp.zeros((windows, channels), jnp.float32)
+    for part in range(2):
+        for f in range(bins):
+            v = spectra_ref[part, f].astype(jnp.float32)
+            power = power + v * v
+    power = power / bins
+    factor = alive_ref[...].astype(jnp.float32) / jnp.sqrt(jnp.maximum(power, 0.5))
+
+    peers = 3 + jnp.where(z < n_z - 1, 1, 0) + jnp.where(z > 0, 1, 0)
+    pl.semaphore_wait(barrier, peers)
+
+    def remote(src, dst, send, recv, target):
+        return pltpu.make_async_remote_copy(
+            src_ref=src,
+            dst_ref=dst,
+            send_sem=send,
+            recv_sem=recv,
+            device_id=target,
+            device_id_type=MESH,
+        )
+
+    def to_sib(f):
+        return remote(col.at[f, s], col.at[f, s], s_sib.at[f], r_sib.at[f], (sib, r))
+
+    def to_x(f):
+        return remote(col.at[f, s], col.at[f, s], s_x.at[f], r_x.at[f], (xp, r))
+
+    def fwd(f):
+        return remote(col.at[f, xp], col.at[f, xp], s_fwd.at[f], r_fwd.at[f], (sib, r))
+
+    def to_up(f):
+        return remote(srcs.at[y, f], srcs.at[y, f], s_up.at[f], r_own.at[f], (s, r + 2))
+
+    def to_dn(f):
+        return remote(srcs.at[y, f], srcs.at[y, f], s_dn.at[f], r_own.at[f], (s, r - 2))
+
+    def to_y(f):
+        return remote(srcs.at[y, f], srcs.at[y, f], s_y.at[f], r_oth.at[f], (s, ry))
+
+    def arrived(ref, sem):
+        remote(ref, ref, sem, sem, (sib, r)).wait_recv()
+
+    def put(f, half):
+        rows = pl.ds(pl.multiple_of(half * channels, channels), channels)
+        return pltpu.make_async_copy(
+            stage.at[f, half], out_ref.at[:, f, rows, :], o_sem.at[f, half]
+        )
+
+    for f in range(bins):
+        for part in range(2):
+            v = spectra_ref[part, f].astype(jnp.float32)
+            col[f, s, part] = (v * factor).astype(jnp.bfloat16)
+        to_x(f).start()
+        to_sib(f).start()
+
+    n_src = col.shape[1]
+    depth = n_src * 2 * windows
+    scale = jnp.float32(1.0) / jnp.sqrt(jnp.float32(n_src * windows))
+
+    def multiply(f, half):
+        left = srcs[half, f].reshape(depth, channels)
+        acc = lax.dot_general(
+            left,
+            rhs[...].reshape(depth, 2 * channels),
+            (((0,), (0,)), ((), ())),
+            preferred_element_type=jnp.float32,
+        )
+        acc = (acc * scale).astype(jnp.bfloat16)
+        stage[f, half, 0] = acc[:, :channels]
+        stage[f, half, 1] = acc[:, channels:]
+        put(f, half).start()
+
+    def step(f, carry):
+        @pl.when(f < bins)
+        def _():
+            arrived(col.at[f, xp], r_x.at[f])
+            fwd(f).start()
+            arrived(col.at[f, sib], r_sib.at[f])
+            arrived(col.at[f, diag], r_fwd.at[f])
+
+            @pl.when(is_root)
+            def _():
+                srcs[y, f] = col[f]
+
+            @pl.when(jnp.logical_not(is_root))
+            def _():
+                arrived(srcs.at[y, f], r_own.at[f])
+
+            @pl.when(up_ok)
+            def _():
+                to_up(f).start()
+
+            @pl.when(dn_ok)
+            def _():
+                to_dn(f).start()
+
+            to_y(f).start()
+
+        @pl.when(f >= 1)
+        def _():
+            g = f - 1
+            whole = col[g]
+            rhs[:, :, :, :channels] = whole
+            rhs[:, 0, :, channels:] = whole[:, 1]
+            rhs[:, 1, :, channels:] = -whole[:, 0]
+            multiply(g, y)
+            arrived(srcs.at[oy, g], r_oth.at[g])
+            multiply(g, oy)
+
+        return carry
+
+    lax.fori_loop(0, bins + 1, step, 0)
+
+    def drain(f, carry):
+        to_sib(f).wait_send()
+        to_x(f).wait_send()
+        fwd(f).wait_send()
+        to_y(f).wait_send()
+
+        @pl.when(up_ok)
+        def _():
+            to_up(f).wait_send()
+
+        @pl.when(dn_ok)
+        def _():
+            to_dn(f).wait_send()
+
+        put(f, 0).wait()
+        put(f, 1).wait()
+        return carry
+
+    lax.fori_loop(0, bins, drain, 0)
+
+
+def grid_body(n_z, spectra, alive):
+    parts, bins, windows, channels = spectra.shape
+    n_src = lax.axis_size("src")
+    dma = pltpu.SemaphoreType.DMA
+    rows = 2 * channels
+    return pl.pallas_call(
+        functools.partial(kernel, n_z),
+        out_shape=jax.ShapeDtypeStruct((parts, bins, rows, channels), jnp.bfloat16),
+        in_specs=[pl.BlockSpec(memory_space=pltpu.VMEM)] * 2,
+        out_specs=pl.BlockSpec(memory_space=pl.ANY),
+        scratch_shapes=[
+            pltpu.VMEM((bins, n_src, parts, windows, channels), jnp.bfloat16),
+            pltpu.VMEM((2, bins, n_src, parts, windows, channels), jnp.bfloat16),
+            pltpu.VMEM((n_src, parts, windows, 2 * channels), jnp.bfloat16),
+            pltpu.VMEM((bins, 2, parts, channels, channels), jnp.bfloat16),
+        ]
+        + [dma((bins,))] * 11
+        + [dma((bins, 2))],
+        compiler_params=pltpu.CompilerParams(
+            collective_id=0, has_side_effects=True, vmem_limit_bytes=48 * 2**20
+        ),
+        cost_estimate=pl.CostEstimate(
+            flops=8 * bins * n_src * windows * rows * channels,
+            bytes_accessed=10 * spectra.size * parts * n_src,
+            transcendentals=0,
+        ),
+    )(spectra, alive)
+
+
 def solution(mesh):
+    if mesh.shape["src"] == 4 and mesh.shape["rcv"] == 8:
+        body = functools.partial(grid_body, mesh.shape["rcv"] // 2)
+    else:
+        body = general_body
     return jax.shard_map(
         body,
         mesh=mesh,

time: 180 us -> 70.8 us (0.39)
  waiting for transfers between devices: 151 us -> 0 us
  Pallas kernels: 0 us -> 66.3 us
  between operations: 13.5 us -> 0.01 us
  other arithmetic: 9.79 us -> 0 us
  matrix products: 2.88 us -> 0 us
  local copies, waits for them, and re-layouts: 2.01 us -> 3.81 us
    psum x1 -> x0, waiting for transfers between devices: 130 us -> none  [spread(): return lax.psum(block, axis)]
    pallas_call x0 -> x1, Pallas kernels: none -> 66.3 us  [grid_body(): pl.pallas_call(functools.partial(kernel, n_z), out_shape=jax.ShapeDtypeSt...]
    all_gather x1 -> x0, waiting for transfers between devices: 20.2 us -> none  [body(): receivers = lax.all_gather(whitened, 'src', axis=2, tiled=True)]
    convert_element_type x2 -> x0, other arithmetic: 4.38 us -> none  [the longest x1 2.55 us: body(): return (stacked * factor).astype(jnp.bfloat16)]
    select_n x1 -> x0, other arithmetic: 3.41 us -> none  [spread(): jnp.where(lax.axis_index(axis) == holder, block, jnp.zeros_like(block))]
    dot_general x2 -> x0, matrix products: 2.88 us -> none  [the longest x1 1.45 us: cross_terms(): jnp.einsum('kfwc,kfwd->fcd', source_part, swapped, preferred_element_type...]
    unnamed x5, local copies, waits for them, and re-layouts: 1.88 us -> 3.81 us
  transfers between devices with their start and end apart: 2 -> 0, of which waited for: 2 -> 0; matrix products, arithmetic and copies ran while one was open for 0% -> 0% of each run, Pallas kernels for 0% -> 0%
where the time goes in v1:
time: 70.8 us; the launch traced here: 70.1 us
  Pallas kernels  66.3 us (94%)
  local copies, waits for them, and re-layouts  3.81 us (5%)
    pallas_call x1, Pallas kernels, grid_body(): pl.pallas_call(functools.partial(kernel, n_z), out_shape=jax.ShapeDtypeSt...  66.3 us
    unnamed x5, local copies, waits for them, and re-layouts  3.81 us

profile of v1, /device:TPU:3, one launch (start us, length us, event | category | flops | bytes accessed | tf_op | source)
XLA Modules:
  0.0 70.1 jit_solution(16385051584706712394)
XLA Ops:
  0.0 0.0 copy-start
  0.0 1.0 %copy-done = bf16[2,8,48,256]{3,2,1,0:T(8,128)(2,1)S(1)} copy-done((bf16[2,8,48,256]{3,2,1,0:T(8,128)(2,1)S(1)}, bf16[2,8,48,256]{3,2,1,0:T(8,128)(2,1)}, u32[]{:S(2)}) %copy-start) | copy-done | bytes 393240
  1.0 0.0 copy-start.1
  1.0 0.8 %copy-done.1 = s32[48,256]{1,0:T(8,128)S(1)} copy-done((s32[48,256]{1,0:T(8,128)S(1)}, s32[48,256]{1,0:T(8,128)}, u32[]{:S(2)}) %copy-start.1) | copy-done | bytes 49176
  1.8 66.3 %shard_map.28 = bf16[2,8,512,256]{3,2,1,0:T(8,128)(2,1)S(1)} custom-call(bf16[2,8,48,256]{3,2,1,0:T(8,128)(2,1)S(1)} %copy-done, s32[48,256]{1,0:T(8,128)S(1)} %copy-done.1), custom_call_target="tpu_custom_call" | custom-call | flops 1610612736 | bytes 15728640 | tf_op jit(solution)/shard_map/pallas_call | solution.py:242
  68.1 2.0 %copy.4 = bf16[2,8,512,256]{3,2,1,0:T(8,128)(2,1)} copy(bf16[2,8,512,256]{3,2,1,0:T(8,128)(2,1)S(1)} %shard_map.28) | data formatting | bytes 8388608
Async XLA Ops:
  0.0 1.0 %copy-start = (bf16[2,8,48,256]{3,2,1,0:T(8,128)(2,1)S(1)}, bf16[2,8,48,256]{3,2,1,0:T(8,128)(2,1)}, u32[]{:S(2)}) copy-start(bf16[2,8,48,256]{3,2,1,0:T(8,128)(2,1)} %spectra_ref.1) | copy-start | bytes 1179652
  1.0 0.8 %copy-start.1 = (s32[48,256]{1,0:T(8,128)S(1)}, s32[48,256]{1,0:T(8,128)}, u32[]{:S(2)}) copy-start(s32[48,256]{1,0:T(8,128)} %alive_ref.1) | copy-start | bytes 147460

commit v2 on v1

--- a/solution.py
+++ b/solution.py
@@ -9,8 +9,7 @@
 
 MESH = pl.DeviceIdType.MESH
 
-N_VIA_X = 0
-N_Y_ONCE = 0
+N_Y_ONCE = 2
 
 
 def spread(block, axis, holder):
@@ -54,39 +53,61 @@
 
 def kernel(
     n_z,
+    spectra_hbm,
+    alive_hbm,
+    out_ref,
     spectra_ref,
     alive_ref,
-    out_ref,
     col,
     srcs,
+    transit,
     rhs,
     stage,
     r_sib,
     r_x,
     r_fwd,
-    r_own,
-    r_oth,
+    r_z,
+    r_t,
+    r_tx,
+    r_ya,
+    r_yb,
     s_sib,
     s_x,
     s_fwd,
     s_up,
     s_dn,
-    s_y,
+    s_tup,
+    s_tdn,
+    s_tx,
+    s_ya,
+    s_yb,
+    s_up2,
+    s_dn2,
+    i_sem,
     o_sem,
 ):
     bins, windows, channels = spectra_ref.shape[1:]
     s = lax.axis_index("src")
     r = lax.axis_index("rcv")
+    x = s // 2
+    core = lax.rem(s, 2)
     y = lax.rem(r, 2)
     z = r // 2
-    sib = s + 1 - 2 * lax.rem(s, 2)
-    xp = lax.rem(s + 2, 4)
-    diag = lax.rem(sib + 2, 4)
+    ox, ocore, oy = 1 - x, 1 - core, 1 - y
+    sib = 2 * x + ocore
+    xp = 2 * ox + core
     ry = r + 1 - 2 * y
-    oy = 1 - y
     is_root = z == s
+    is_troot = z == xp
     up_ok = jnp.logical_and(z >= s, z < n_z - 1)
     dn_ok = jnp.logical_and(z <= s, z > 0)
+    tup_ok = jnp.logical_and(z >= xp, z < n_z - 1)
+    tdn_ok = jnp.logical_and(z <= xp, z > 0)
+
+    load_spectra = pltpu.make_async_copy(spectra_hbm, spectra_ref, i_sem.at[0])
+    load_alive = pltpu.make_async_copy(alive_hbm, alive_ref, i_sem.at[1])
+    load_spectra.start()
+    load_alive.start()
 
     barrier = pltpu.get_barrier_semaphore()
     for target in ((sib, r), (xp, r), (s, ry)):
@@ -100,6 +121,8 @@
     def _():
         pl.semaphore_signal(barrier, inc=1, device_id=(s, r - 2), device_id_type=MESH)
 
+    load_spectra.wait()
+    load_alive.wait()
     power = jnp.zeros((windows, channels), jnp.float32)
     for part in range(2):
         for f in range(bins):
@@ -121,23 +144,53 @@
             device_id_type=MESH,
         )
 
+    above, below, across = (s, r + 2), (s, r - 2), (s, ry)
+
     def to_sib(f):
-        return remote(col.at[f, s], col.at[f, s], s_sib.at[f], r_sib.at[f], (sib, r))
+        block = col.at[f, x, core]
+        return remote(block, block, s_sib.at[f], r_sib.at[f], (sib, r))
 
     def to_x(f):
-        return remote(col.at[f, s], col.at[f, s], s_x.at[f], r_x.at[f], (xp, r))
+        block = col.at[f, x, core]
+        return remote(block, block, s_x.at[f], r_x.at[f], (xp, r))
 
     def fwd(f):
-        return remote(col.at[f, xp], col.at[f, xp], s_fwd.at[f], r_fwd.at[f], (sib, r))
+        block = col.at[f, ox, core]
+        return remote(block, block, s_fwd.at[f], r_fwd.at[f], (sib, r))
 
     def to_up(f):
-        return remote(srcs.at[y, f], srcs.at[y, f], s_up.at[f], r_own.at[f], (s, r + 2))
+        block = srcs.at[y, f, x]
+        return remote(block, block, s_up.at[f], r_z.at[f], above)
 
     def to_dn(f):
-        return remote(srcs.at[y, f], srcs.at[y, f], s_dn.at[f], r_own.at[f], (s, r - 2))
-
-    def to_y(f):
-        return remote(srcs.at[y, f], srcs.at[y, f], s_y.at[f], r_oth.at[f], (s, ry))
+        block = srcs.at[y, f, x]
+        return remote(block, block, s_dn.at[f], r_z.at[f], below)
+
+    def to_ya(f):
+        block = srcs.at[y, f, x]
+        return remote(block, block, s_ya.at[f], r_ya.at[f], across)
+
+    def to_yb(f):
+        block = srcs.at[y, f, ox]
+        return remote(block, block, s_yb.at[f], r_yb.at[f], across)
+
+    def to_up2(f):
+        block = srcs.at[oy, f, x]
+        return remote(block, block, s_up2.at[f], r_ya.at[f], above)
+
+    def to_dn2(f):
+        block = srcs.at[oy, f, x]
+        return remote(block, block, s_dn2.at[f], r_ya.at[f], below)
+
+    def to_tup(f):
+        return remote(transit.at[f], transit.at[f], s_tup.at[f], r_t.at[f], above)
+
+    def to_tdn(f):
+        return remote(transit.at[f], transit.at[f], s_tdn.at[f], r_t.at[f], below)
+
+    def to_tx(f):
+        block = srcs.at[y, f, x]
+        return remote(transit.at[f], block, s_tx.at[f], r_tx.at[f], (xp, r))
 
     def arrived(ref, sem):
         remote(ref, ref, sem, sem, (sib, r)).wait_recv()
@@ -151,18 +204,17 @@
     for f in range(bins):
         for part in range(2):
             v = spectra_ref[part, f].astype(jnp.float32)
-            col[f, s, part] = (v * factor).astype(jnp.bfloat16)
+            col[f, x, core, part] = (v * factor).astype(jnp.bfloat16)
+        to_sib(f).start()
         to_x(f).start()
-        to_sib(f).start()
-
-    n_src = col.shape[1]
+
+    n_src = col.shape[1] * col.shape[2]
     depth = n_src * 2 * windows
     scale = jnp.float32(1.0) / jnp.sqrt(jnp.float32(n_src * windows))
 
     def multiply(f, half):
-        left = srcs[half, f].reshape(depth, channels)
         acc = lax.dot_general(
-            left,
+            srcs[half, f].reshape(depth, channels),
             rhs[...].reshape(depth, 2 * channels),
             (((0,), (0,)), ((), ())),
             preferred_element_type=jnp.float32,
@@ -172,60 +224,123 @@
         stage[f, half, 1] = acc[:, channels:]
         put(f, half).start()
 
+    def both(first, second):
+        return jnp.logical_and(first, second)
+
+    def send_along(f):
+        arrived(col.at[f, x, ocore], r_sib.at[f])
+
+        @pl.when(is_root)
+        def _():
+            srcs[y, f, x] = col[f, x]
+
+        @pl.when(jnp.logical_not(is_root))
+        def _():
+            arrived(srcs.at[y, f, x], r_z.at[f])
+
+        @pl.when(up_ok)
+        def _():
+            to_up(f).start()
+
+        @pl.when(dn_ok)
+        def _():
+            to_dn(f).start()
+
+        @pl.when(jnp.logical_or(is_root, f >= N_Y_ONCE))
+        def _():
+            to_ya(f).start()
+
+        @pl.when(is_troot)
+        def _():
+            transit[f] = col[f, x]
+
+        @pl.when(jnp.logical_not(is_troot))
+        def _():
+            arrived(transit.at[f], r_t.at[f])
+
+        @pl.when(tup_ok)
+        def _():
+            to_tup(f).start()
+
+        @pl.when(tdn_ok)
+        def _():
+            to_tdn(f).start()
+
+        @pl.when(jnp.logical_not(is_troot))
+        def _():
+            to_tx(f).start()
+
+        arrived(col.at[f, ox, core], r_x.at[f])
+        fwd(f).start()
+
+    def send_across(f):
+        arrived(col.at[f, ox, ocore], r_fwd.at[f])
+
+        @pl.when(is_root)
+        def _():
+            srcs[y, f, ox] = col[f, ox]
+
+        @pl.when(jnp.logical_not(is_root))
+        def _():
+            arrived(srcs.at[y, f, ox], r_tx.at[f])
+
+        to_yb(f).start()
+        arrived(srcs.at[oy, f, x], r_ya.at[f])
+
+        @pl.when(both(up_ok, f < N_Y_ONCE))
+        def _():
+            to_up2(f).start()
+
+        @pl.when(both(dn_ok, f < N_Y_ONCE))
+        def _():
+            to_dn2(f).start()
+
+    def finish(f):
+        whole = col[f]
+        rhs[:, :, :, :, :channels] = whole
+        rhs[:, :, 0, :, channels:] = whole[:, :, 1]
+        rhs[:, :, 1, :, channels:] = -whole[:, :, 0]
+        multiply(f, y)
+        arrived(srcs.at[oy, f, ox], r_yb.at[f])
+        multiply(f, oy)
+
     def step(f, carry):
         @pl.when(f < bins)
         def _():
-            arrived(col.at[f, xp], r_x.at[f])
-            fwd(f).start()
-            arrived(col.at[f, sib], r_sib.at[f])
-            arrived(col.at[f, diag], r_fwd.at[f])
-
-            @pl.when(is_root)
-            def _():
-                srcs[y, f] = col[f]
-
-            @pl.when(jnp.logical_not(is_root))
-            def _():
-                arrived(srcs.at[y, f], r_own.at[f])
-
-            @pl.when(up_ok)
-            def _():
-                to_up(f).start()
-
-            @pl.when(dn_ok)
-            def _():
-                to_dn(f).start()
-
-            to_y(f).start()
-
-        @pl.when(f >= 1)
-        def _():
-            g = f - 1
-            whole = col[g]
-            rhs[:, :, :, :channels] = whole
-            rhs[:, 0, :, channels:] = whole[:, 1]
-            rhs[:, 1, :, channels:] = -whole[:, 0]
-            multiply(g, y)
-            arrived(srcs.at[oy, g], r_oth.at[g])
-            multiply(g, oy)
+            send_along(f)
+
+        @pl.when(both(f >= 1, f < bins + 1))
+        def _():
+            send_across(f - 1)
+
+        @pl.when(f >= 2)
+        def _():
+            finish(f - 2)
 
         return carry
 
-    lax.fori_loop(0, bins + 1, step, 0)
+    lax.fori_loop(0, bins + 2, step, 0)
 
     def drain(f, carry):
         to_sib(f).wait_send()
         to_x(f).wait_send()
         fwd(f).wait_send()
-        to_y(f).wait_send()
-
-        @pl.when(up_ok)
-        def _():
-            to_up(f).wait_send()
-
-        @pl.when(dn_ok)
-        def _():
-            to_dn(f).wait_send()
+        to_yb(f).wait_send()
+
+        for sent, condition in (
+            (to_up, up_ok),
+            (to_dn, dn_ok),
+            (to_ya, jnp.logical_or(is_root, f >= N_Y_ONCE)),
+            (to_tup, tup_ok),
+            (to_tdn, tdn_ok),
+            (to_tx, jnp.logical_not(is_troot)),
+            (to_up2, both(up_ok, f < N_Y_ONCE)),
+            (to_dn2, both(dn_ok, f < N_Y_ONCE)),
+        ):
+
+            @pl.when(condition)
+            def _(sent=sent):
+                sent(f).wait_send()
 
         put(f, 0).wait()
         put(f, 1).wait()
@@ -239,19 +354,23 @@
     n_src = lax.axis_size("src")
     dma = pltpu.SemaphoreType.DMA
     rows = 2 * channels
+    block = (2, parts, windows, channels)
     return pl.pallas_call(
         functools.partial(kernel, n_z),
         out_shape=jax.ShapeDtypeStruct((parts, bins, rows, channels), jnp.bfloat16),
-        in_specs=[pl.BlockSpec(memory_space=pltpu.VMEM)] * 2,
+        in_specs=[pl.BlockSpec(memory_space=pl.ANY)] * 2,
         out_specs=pl.BlockSpec(memory_space=pl.ANY),
         scratch_shapes=[
-            pltpu.VMEM((bins, n_src, parts, windows, channels), jnp.bfloat16),
-            pltpu.VMEM((2, bins, n_src, parts, windows, channels), jnp.bfloat16),
-            pltpu.VMEM((n_src, parts, windows, 2 * channels), jnp.bfloat16),
+            pltpu.VMEM(spectra.shape, jnp.bfloat16),
+            pltpu.VMEM(alive.shape, jnp.int32),
+            pltpu.VMEM((bins, 2) + block, jnp.bfloat16),
+            pltpu.VMEM((2, bins, 2) + block, jnp.bfloat16),
+            pltpu.VMEM((bins,) + block, jnp.bfloat16),
+            pltpu.VMEM((2, 2, parts, windows, 2 * channels), jnp.bfloat16),
             pltpu.VMEM((bins, 2, parts, channels, channels), jnp.bfloat16),
         ]
-        + [dma((bins,))] * 11
-        + [dma((bins, 2))],
+        + [dma((bins,))] * 20
+        + [dma((2,)), dma((bins, 2))],
         compiler_params=pltpu.CompilerParams(
             collective_id=0, has_side_effects=True, vmem_limit_bytes=48 * 2**20
         ),

time: 70.8 us -> 143 us (2.02)
  the two profiles are of different devices: /device:TPU:3 before, /device:TPU:24 now
where the time goes in v2:
time: 143 us
  Pallas kernels  139 us (97%)
  local copies, waits for them, and re-layouts  3.81 us (3%)
    pallas_call x1, Pallas kernels, grid_body(): pl.pallas_call(functools.partial(kernel, n_z), out_shape=jax.ShapeDtypeSt...  139 us
    unnamed x5, local copies, waits for them, and re-layouts  3.81 us

profile of v2, /device:TPU:24, one launch (start us, length us, event | category | flops | bytes accessed | tf_op | source)
XLA Modules:
  0.0 142.8 jit_solution(14306603955783441622)
XLA Ops:
  0.0 0.0 copy-start
  0.0 1.0 copy-done
  1.0 0.0 copy-start.1
  1.0 0.8 copy-done.1
  1.8 139.0 %shard_map.28 = bf16[2,8,512,256]{3,2,1,0:T(8,128)(2,1)S(1)} custom-call(bf16[2,8,48,256]{3,2,1,0:T(8,128)(2,1)S(1)} %copy-done, s32[48,256]{1,0:T(8,128)S(1)} %copy-done.1), custom_call_target="tpu_custom_call" | custom-call | flops 1610612736 | bytes 15728640 | tf_op jit(solution)/shard_map/pallas_call | solution.py:358
  140.8 2.0 %copy.4 = bf16[2,8,512,256]{3,2,1,0:T(8,128)(2,1)} copy(bf16[2,8,512,256]{3,2,1,0:T(8,128)(2,1)S(1)} %shard_map.28) | data formatting | bytes 8388608
Async XLA Ops:
  0.0 1.0 copy-start
  1.0 0.8 copy-start.1

commit v3 on v2

--- a/solution.py
+++ b/solution.py
@@ -10,6 +10,7 @@
 MESH = pl.DeviceIdType.MESH
 
 N_Y_ONCE = 2
+HOP = 2
 
 
 def spread(block, axis, holder):
@@ -227,11 +228,10 @@
     def both(first, second):
         return jnp.logical_and(first, second)
 
-    def send_along(f):
-        arrived(col.at[f, x, ocore], r_sib.at[f])
-
+    def along_own(f):
         @pl.when(is_root)
         def _():
+            arrived(col.at[f, x, ocore], r_sib.at[f])
             srcs[y, f, x] = col[f, x]
 
         @pl.when(jnp.logical_not(is_root))
@@ -250,8 +250,10 @@
         def _():
             to_ya(f).start()
 
+    def along_transit(f):
         @pl.when(is_troot)
         def _():
+            arrived(col.at[f, x, ocore], r_sib.at[f])
             transit[f] = col[f, x]
 
         @pl.when(jnp.logical_not(is_troot))
@@ -270,14 +272,14 @@
         def _():
             to_tx(f).start()
 
+    def column(f):
         arrived(col.at[f, ox, core], r_x.at[f])
         fwd(f).start()
 
-    def send_across(f):
-        arrived(col.at[f, ox, ocore], r_fwd.at[f])
-
+    def across_other(f):
         @pl.when(is_root)
         def _():
+            arrived(col.at[f, ox, ocore], r_fwd.at[f])
             srcs[y, f, ox] = col[f, ox]
 
         @pl.when(jnp.logical_not(is_root))
@@ -285,17 +287,31 @@
             arrived(srcs.at[y, f, ox], r_tx.at[f])
 
         to_yb(f).start()
+
+    def across_once(f):
         arrived(srcs.at[oy, f, x], r_ya.at[f])
 
-        @pl.when(both(up_ok, f < N_Y_ONCE))
+        @pl.when(up_ok)
         def _():
             to_up2(f).start()
 
-        @pl.when(both(dn_ok, f < N_Y_ONCE))
+        @pl.when(dn_ok)
         def _():
             to_dn2(f).start()
 
     def finish(f):
+        @pl.when(jnp.logical_not(jnp.logical_or(is_root, is_troot)))
+        def _():
+            arrived(col.at[f, x, ocore], r_sib.at[f])
+
+        @pl.when(jnp.logical_not(is_root))
+        def _():
+            arrived(col.at[f, ox, ocore], r_fwd.at[f])
+
+        @pl.when(f >= N_Y_ONCE)
+        def _():
+            arrived(srcs.at[oy, f, x], r_ya.at[f])
+
         whole = col[f]
         rhs[:, :, :, :, :channels] = whole
         rhs[:, :, 0, :, channels:] = whole[:, :, 1]
@@ -304,22 +320,29 @@
         arrived(srcs.at[oy, f, ox], r_yb.at[f])
         multiply(f, oy)
 
-    def step(f, carry):
-        @pl.when(f < bins)
-        def _():
-            send_along(f)
-
-        @pl.when(both(f >= 1, f < bins + 1))
-        def _():
-            send_across(f - 1)
-
-        @pl.when(f >= 2)
-        def _():
-            finish(f - 2)
+    dist = HOP * jnp.where(z > s, z - s, s - z)
+    tdist = HOP * jnp.where(z > xp, z - xp, xp - z)
+    b_lag = HOP + jnp.where(is_root, HOP, dist)
+    last = b_lag + HOP
+    n_steps = bins + HOP * (n_z + 1)
+
+    def step(t, carry):
+        for work, lag, count in (
+            (along_own, dist, bins),
+            (along_transit, tdist, bins),
+            (column, 1, bins),
+            (across_once, dist + HOP, N_Y_ONCE),
+            (across_other, b_lag, bins),
+            (finish, last, bins),
+        ):
+
+            @pl.when(both(t >= lag, t < lag + count))
+            def _(work=work, lag=lag):
+                work(t - lag)
 
         return carry
 
-    lax.fori_loop(0, bins + 2, step, 0)
+    lax.fori_loop(0, n_steps, step, 0)
 
     def drain(f, carry):
         to_sib(f).wait_send()

time: 143 us -> 57.4 us (0.40)
  the two profiles are of different devices: /device:TPU:24 before, /device:TPU:3 now
where the time goes in v3:
time: 57.4 us; the launch traced here: 57.2 us
  Pallas kernels  53.3 us (93%)
  local copies, waits for them, and re-layouts  3.81 us (7%)
    pallas_call x1, Pallas kernels, grid_body(): pl.pallas_call(functools.partial(kernel, n_z), out_shape=jax.ShapeDtypeSt...  53.3 us
    unnamed x5, local copies, waits for them, and re-layouts  3.81 us

profile of v3, /device:TPU:3, one launch (start us, length us, event | category | flops | bytes accessed | tf_op | source)
XLA Modules:
  0.0 57.2 jit_solution(6591304196718850033)
XLA Ops:
  0.0 0.0 copy-start
  0.0 1.0 %copy-done = bf16[2,8,48,256]{3,2,1,0:T(8,128)(2,1)S(1)} copy-done((bf16[2,8,48,256]{3,2,1,0:T(8,128)(2,1)S(1)}, bf16[2,8,48,256]{3,2,1,0:T(8,128)(2,1)}, u32[]{:S(2)}) %copy-start) | copy-done | bytes 393240
  1.0 0.0 copy-start.1
  1.0 0.8 %copy-done.1 = s32[48,256]{1,0:T(8,128)S(1)} copy-done((s32[48,256]{1,0:T(8,128)S(1)}, s32[48,256]{1,0:T(8,128)}, u32[]{:S(2)}) %copy-start.1) | copy-done | bytes 49176
  1.8 53.3 %shard_map.28 = bf16[2,8,512,256]{3,2,1,0:T(8,128)(2,1)S(1)} custom-call(bf16[2,8,48,256]{3,2,1,0:T(8,128)(2,1)S(1)} %copy-done, s32[48,256]{1,0:T(8,128)S(1)} %copy-done.1), custom_call_target="tpu_custom_call" | custom-call | flops 1610612736 | bytes 15728640 | tf_op jit(solution)/shard_map/pallas_call | solution.py:381
  55.1 2.0 %copy.4 = bf16[2,8,512,256]{3,2,1,0:T(8,128)(2,1)} copy(bf16[2,8,512,256]{3,2,1,0:T(8,128)(2,1)S(1)} %shard_map.28) | data formatting | bytes 8388608
Async XLA Ops:
  0.0 1.0 %copy-start = (bf16[2,8,48,256]{3,2,1,0:T(8,128)(2,1)S(1)}, bf16[2,8,48,256]{3,2,1,0:T(8,128)(2,1)}, u32[]{:S(2)}) copy-start(bf16[2,8,48,256]{3,2,1,0:T(8,128)(2,1)} %spectra_hbm.1) | copy-start | bytes 1179652
  1.0 0.8 %copy-start.1 = (s32[48,256]{1,0:T(8,128)S(1)}, s32[48,256]{1,0:T(8,128)}, u32[]{:S(2)}) copy-start(s32[48,256]{1,0:T(8,128)} %alive_hbm.1) | copy-start | bytes 147460

commit v4 on v3

--- a/solution.py
+++ b/solution.py
@@ -9,8 +9,8 @@
 
 MESH = pl.DeviceIdType.MESH
 
-N_Y_ONCE = 2
-HOP = 2
+N_Y_ONCE = 4
+HOP = 3
 
 
 def spread(block, axis, holder):
@@ -88,6 +88,7 @@
     o_sem,
 ):
     bins, windows, channels = spectra_ref.shape[1:]
+    chunks = 2 * bins
     s = lax.axis_index("src")
     r = lax.axis_index("rcv")
     x = s // 2
@@ -205,9 +206,9 @@
     for f in range(bins):
         for part in range(2):
             v = spectra_ref[part, f].astype(jnp.float32)
-            col[f, x, core, part] = (v * factor).astype(jnp.bfloat16)
-        to_sib(f).start()
-        to_x(f).start()
+            col[2 * f + part, x, core] = (v * factor).astype(jnp.bfloat16)
+            to_sib(2 * f + part).start()
+            to_x(2 * f + part).start()
 
     n_src = col.shape[1] * col.shape[2]
     depth = n_src * 2 * windows
@@ -215,7 +216,7 @@
 
     def multiply(f, half):
         acc = lax.dot_general(
-            srcs[half, f].reshape(depth, channels),
+            srcs[half, pl.ds(2 * f, 2)].reshape(depth, channels),
             rhs[...].reshape(depth, 2 * channels),
             (((0,), (0,)), ((), ())),
             preferred_element_type=jnp.float32,
@@ -312,28 +313,32 @@
         def _():
             arrived(srcs.at[oy, f, x], r_ya.at[f])
 
-        whole = col[f]
-        rhs[:, :, :, :, :channels] = whole
-        rhs[:, :, 0, :, channels:] = whole[:, :, 1]
-        rhs[:, :, 1, :, channels:] = -whole[:, :, 0]
-        multiply(f, y)
         arrived(srcs.at[oy, f, ox], r_yb.at[f])
-        multiply(f, oy)
+
+        @pl.when(lax.rem(f, 2) == 1)
+        def _():
+            real, imag = col[f - 1], col[f]
+            rhs[0, :, :, :, :channels] = real
+            rhs[1, :, :, :, :channels] = imag
+            rhs[0, :, :, :, channels:] = imag
+            rhs[1, :, :, :, channels:] = -real
+            multiply(f // 2, 0)
+            multiply(f // 2, 1)
 
     dist = HOP * jnp.where(z > s, z - s, s - z)
     tdist = HOP * jnp.where(z > xp, z - xp, xp - z)
     b_lag = HOP + jnp.where(is_root, HOP, dist)
     last = b_lag + HOP
-    n_steps = bins + HOP * (n_z + 1)
+    n_steps = chunks + HOP * (n_z + 1)
 
     def step(t, carry):
         for work, lag, count in (
-            (along_own, dist, bins),
-            (along_transit, tdist, bins),
-            (column, 1, bins),
+            (along_own, dist, chunks),
+            (along_transit, tdist, chunks),
+            (column, 1, chunks),
             (across_once, dist + HOP, N_Y_ONCE),
-            (across_other, b_lag, bins),
-            (finish, last, bins),
+            (across_other, b_lag, chunks),
+            (finish, last, chunks),
         ):
 
             @pl.when(both(t >= lag, t < lag + count))
@@ -365,11 +370,16 @@
             def _(sent=sent):
                 sent(f).wait_send()
 
+        return carry
+
+    lax.fori_loop(0, chunks, drain, 0)
+
+    def stored(f, carry):
         put(f, 0).wait()
         put(f, 1).wait()
         return carry
 
-    lax.fori_loop(0, bins, drain, 0)
+    lax.fori_loop(0, bins, stored, 0)
 
 
 def grid_body(n_z, spectra, alive):
@@ -377,7 +387,8 @@
     n_src = lax.axis_size("src")
     dma = pltpu.SemaphoreType.DMA
     rows = 2 * channels
-    block = (2, parts, windows, channels)
+    block = (2, windows, channels)
+    chunks = parts * bins
     return pl.pallas_call(
         functools.partial(kernel, n_z),
         out_shape=jax.ShapeDtypeStruct((parts, bins, rows, channels), jnp.bfloat16),
@@ -386,16 +397,16 @@
         scratch_shapes=[
             pltpu.VMEM(spectra.shape, jnp.bfloat16),
             pltpu.VMEM(alive.shape, jnp.int32),
-            pltpu.VMEM((bins, 2) + block, jnp.bfloat16),
-            pltpu.VMEM((2, bins, 2) + block, jnp.bfloat16),
-            pltpu.VMEM((bins,) + block, jnp.bfloat16),
-            pltpu.VMEM((2, 2, parts, windows, 2 * channels), jnp.bfloat16),
+            pltpu.VMEM((chunks, 2) + block, jnp.bfloat16),
+            pltpu.VMEM((2, chunks, 2) + block, jnp.bfloat16),
+            pltpu.VMEM((chunks,) + block, jnp.bfloat16),
+            pltpu.VMEM((parts, 2, 2, windows, 2 * channels), jnp.bfloat16),
             pltpu.VMEM((bins, 2, parts, channels, channels), jnp.bfloat16),
         ]
-        + [dma((bins,))] * 20
+        + [dma((chunks,))] * 20
         + [dma((2,)), dma((bins, 2))],
         compiler_params=pltpu.CompilerParams(
-            collective_id=0, has_side_effects=True, vmem_limit_bytes=48 * 2**20
+            collective_id=0, has_side_effects=True, vmem_limit_bytes=60 * 2**20
         ),
         cost_estimate=pl.CostEstimate(
             flops=8 * bins * n_src * windows * rows * channels,

time: 57.4 us -> 59 us (1.028)
  Pallas kernels: 53.3 us -> 54.3 us
  local copies, waits for them, and re-layouts: 3.81 us -> 4.57 us
    pallas_call x1, Pallas kernels: 53.3 us -> 54.3 us  [grid_body(): pl.pallas_call(functools.partial(kernel, n_z), out_shape=jax.ShapeDtypeSt...]
    unnamed x5 -> x1, local copies, waits for them, and re-layouts: 3.81 us -> 4.57 us
where the time goes in v4:
time: 59 us; the launch traced here: 58.8 us
  Pallas kernels  54.3 us (92%)
  local copies, waits for them, and re-layouts  4.57 us (8%)
    pallas_call x1, Pallas kernels, grid_body(): pl.pallas_call(functools.partial(kernel, n_z), out_shape=jax.ShapeDtypeSt...  54.3 us
    unnamed x1, local copies, waits for them, and re-layouts  4.57 us

profile of v4, /device:TPU:3, one launch (start us, length us, event | category | flops | bytes accessed | tf_op | source)
XLA Modules:
  0.0 58.8 jit_solution(7077272254492005955)
XLA Ops:
  0.0 54.3 %shard_map.28 = bf16[2,8,512,256]{3,2,1,0:T(8,128)(2,1)} custom-call(bf16[2,8,48,256]{3,2,1,0:T(8,128)(2,1)} %spectra_hbm.1, s32[48,256]{1,0:T(8,128)} %alive_hbm.1), custom_call_target="tpu_custom_call" | custom-call | flops 1610612736 | bytes 15728640 | tf_op jit(solution)/shard_map/pallas_call | solution.py:392
  54.3 4.6 %copy.4 = bf16[2,8,512,256]{3,2,1,0:T(8,128)(2,1)} copy(bf16[2,8,512,256]{3,2,1,0:T(8,128)(2,1)} %shard_map.28) | data formatting | bytes 8388608

commit v5 on v4

--- a/solution.py
+++ b/solution.py
@@ -10,7 +10,7 @@
 MESH = pl.DeviceIdType.MESH
 
 N_Y_ONCE = 4
-HOP = 3
+HOP = 2
 
 
 def spread(block, axis, holder):
@@ -325,23 +325,30 @@
             multiply(f // 2, 0)
             multiply(f // 2, 1)
 
+    @pl.when(is_root)
+    def _():
+        lax.fori_loop(0, chunks, lambda f, carry: (along_own(f), carry)[1], 0)
+
+    @pl.when(is_troot)
+    def _():
+        lax.fori_loop(0, chunks, lambda f, carry: (along_transit(f), carry)[1], 0)
+
     dist = HOP * jnp.where(z > s, z - s, s - z)
     tdist = HOP * jnp.where(z > xp, z - xp, xp - z)
-    b_lag = HOP + jnp.where(is_root, HOP, dist)
-    last = b_lag + HOP
-    n_steps = chunks + HOP * (n_z + 1)
+    b_lag = jnp.where(is_root, HOP, dist)
+    n_steps = chunks + HOP * n_z
 
     def step(t, carry):
-        for work, lag, count in (
-            (along_own, dist, chunks),
-            (along_transit, tdist, chunks),
-            (column, 1, chunks),
-            (across_once, dist + HOP, N_Y_ONCE),
-            (across_other, b_lag, chunks),
-            (finish, last, chunks),
+        for work, lag, count, active in (
+            (along_own, dist - HOP, chunks, jnp.logical_not(is_root)),
+            (along_transit, tdist - HOP, chunks, jnp.logical_not(is_troot)),
+            (column, 0, chunks, True),
+            (across_once, dist, N_Y_ONCE, True),
+            (across_other, b_lag, chunks, True),
+            (finish, b_lag + HOP, chunks, True),
         ):
 
-            @pl.when(both(t >= lag, t < lag + count))
+            @pl.when(both(active, both(t >= lag, t < lag + count)))
             def _(work=work, lag=lag):
                 work(t - lag)
 
@@ -392,7 +399,7 @@
     return pl.pallas_call(
         functools.partial(kernel, n_z),
         out_shape=jax.ShapeDtypeStruct((parts, bins, rows, channels), jnp.bfloat16),
-        in_specs=[pl.BlockSpec(memory_space=pl.ANY)] * 2,
+        in_specs=[pl.BlockSpec(memory_space=pltpu.HBM)] * 2,
         out_specs=pl.BlockSpec(memory_space=pl.ANY),
         scratch_shapes=[
             pltpu.VMEM(spectra.shape, jnp.bfloat16),
@@ -406,7 +413,7 @@
         + [dma((chunks,))] * 20
         + [dma((2,)), dma((bins, 2))],
         compiler_params=pltpu.CompilerParams(
-            collective_id=0, has_side_effects=True, vmem_limit_bytes=60 * 2**20
+            collective_id=0, has_side_effects=True, vmem_limit_bytes=48 * 2**20
         ),
         cost_estimate=pl.CostEstimate(
             flops=8 * bins * n_src * windows * rows * channels,

time: 59 us -> 61.3 us (1.039)
  Pallas kernels: 54.3 us -> 57.3 us
  local copies, waits for them, and re-layouts: 4.57 us -> 3.81 us
    pallas_call x1, Pallas kernels: 54.3 us -> 57.3 us  [grid_body(): pl.pallas_call(functools.partial(kernel, n_z), out_shape=jax.ShapeDtypeSt...]
    unnamed x1 -> x5, local copies, waits for them, and re-layouts: 4.57 us -> 3.81 us
where the time goes in v5:
time: 61.3 us; the launch traced here: 61.1 us
  Pallas kernels  57.3 us (93%)
  local copies, waits for them, and re-layouts  3.81 us (6%)
    pallas_call x1, Pallas kernels, grid_body(): pl.pallas_call(functools.partial(kernel, n_z), out_shape=jax.ShapeDtypeSt...  57.3 us
    unnamed x5, local copies, waits for them, and re-layouts  3.81 us

profile of v5, /device:TPU:3, one launch (start us, length us, event | category | flops | bytes accessed | tf_op | source)
XLA Modules:
  0.0 61.1 jit_solution(234964949294849962)
XLA Ops:
  0.0 0.0 copy-start
  0.0 1.0 %copy-done = bf16[2,8,48,256]{3,2,1,0:T(8,128)(2,1)S(1)} copy-done((bf16[2,8,48,256]{3,2,1,0:T(8,128)(2,1)S(1)}, bf16[2,8,48,256]{3,2,1,0:T(8,128)(2,1)}, u32[]{:S(2)}) %copy-start) | copy-done | bytes 393240
  1.0 0.0 copy-start.1
  1.0 0.8 %copy-done.1 = s32[48,256]{1,0:T(8,128)S(1)} copy-done((s32[48,256]{1,0:T(8,128)S(1)}, s32[48,256]{1,0:T(8,128)}, u32[]{:S(2)}) %copy-start.1) | copy-done | bytes 49176
  1.8 57.3 %shard_map.28 = bf16[2,8,512,256]{3,2,1,0:T(8,128)(2,1)S(1)} custom-call(bf16[2,8,48,256]{3,2,1,0:T(8,128)(2,1)S(1)} %copy-done, s32[48,256]{1,0:T(8,128)S(1)} %copy-done.1), custom_call_target="tpu_custom_call" | custom-call | flops 1610612736 | bytes 15728640 | tf_op jit(solution)/shard_map/pallas_call | solution.py:399
  59.1 2.0 %copy.4 = bf16[2,8,512,256]{3,2,1,0:T(8,128)(2,1)} copy(bf16[2,8,512,256]{3,2,1,0:T(8,128)(2,1)S(1)} %shard_map.28) | data formatting | bytes 8388608
Async XLA Ops:
  0.0 1.0 %copy-start = (bf16[2,8,48,256]{3,2,1,0:T(8,128)(2,1)S(1)}, bf16[2,8,48,256]{3,2,1,0:T(8,128)(2,1)}, u32[]{:S(2)}) copy-start(bf16[2,8,48,256]{3,2,1,0:T(8,128)(2,1)} %spectra_hbm.1) | copy-start | bytes 1179652
  1.0 0.8 %copy-start.1 = (s32[48,256]{1,0:T(8,128)S(1)}, s32[48,256]{1,0:T(8,128)}, u32[]{:S(2)}) copy-start(s32[48,256]{1,0:T(8,128)} %alive_hbm.1) | copy-start | bytes 147460

commit v6 on v4

--- a/solution.py
+++ b/solution.py
@@ -10,7 +10,7 @@
 MESH = pl.DeviceIdType.MESH
 
 N_Y_ONCE = 4
-HOP = 3
+HOP = 2
 
 
 def spread(block, axis, holder):
@@ -54,11 +54,9 @@
 
 def kernel(
     n_z,
-    spectra_hbm,
-    alive_hbm,
-    out_ref,
     spectra_ref,
     alive_ref,
+    out_ref,
     col,
     srcs,
     transit,
@@ -84,7 +82,6 @@
     s_yb,
     s_up2,
     s_dn2,
-    i_sem,
     o_sem,
 ):
     bins, windows, channels = spectra_ref.shape[1:]
@@ -106,11 +103,6 @@
     tup_ok = jnp.logical_and(z >= xp, z < n_z - 1)
     tdn_ok = jnp.logical_and(z <= xp, z > 0)
 
-    load_spectra = pltpu.make_async_copy(spectra_hbm, spectra_ref, i_sem.at[0])
-    load_alive = pltpu.make_async_copy(alive_hbm, alive_ref, i_sem.at[1])
-    load_spectra.start()
-    load_alive.start()
-
     barrier = pltpu.get_barrier_semaphore()
     for target in ((sib, r), (xp, r), (s, ry)):
         pl.semaphore_signal(barrier, inc=1, device_id=target, device_id_type=MESH)
@@ -123,8 +115,6 @@
     def _():
         pl.semaphore_signal(barrier, inc=1, device_id=(s, r - 2), device_id_type=MESH)
 
-    load_spectra.wait()
-    load_alive.wait()
     power = jnp.zeros((windows, channels), jnp.float32)
     for part in range(2):
         for f in range(bins):
@@ -392,11 +382,9 @@
     return pl.pallas_call(
         functools.partial(kernel, n_z),
         out_shape=jax.ShapeDtypeStruct((parts, bins, rows, channels), jnp.bfloat16),
-        in_specs=[pl.BlockSpec(memory_space=pl.ANY)] * 2,
+        in_specs=[pl.BlockSpec(memory_space=pltpu.VMEM)] * 2,
         out_specs=pl.BlockSpec(memory_space=pl.ANY),
         scratch_shapes=[
-            pltpu.VMEM(spectra.shape, jnp.bfloat16),
-            pltpu.VMEM(alive.shape, jnp.int32),
             pltpu.VMEM((chunks, 2) + block, jnp.bfloat16),
             pltpu.VMEM((2, chunks, 2) + block, jnp.bfloat16),
             pltpu.VMEM((chunks,) + block, jnp.bfloat16),
@@ -404,9 +392,9 @@
             pltpu.VMEM((bins, 2, parts, channels, channels), jnp.bfloat16),
         ]
         + [dma((chunks,))] * 20
-        + [dma((2,)), dma((bins, 2))],
+        + [dma((bins, 2))],
         compiler_params=pltpu.CompilerParams(
-            collective_id=0, has_side_effects=True, vmem_limit_bytes=60 * 2**20
+            collective_id=0, has_side_effects=True, vmem_limit_bytes=48 * 2**20
         ),
         cost_estimate=pl.CostEstimate(
             flops=8 * bins * n_src * windows * rows * channels,

time: 59 us -> 57.9 us (0.981)
  local copies, waits for them, and re-layouts: 4.57 us -> 3.81 us
    unnamed x1 -> x5, local copies, waits for them, and re-layouts: 4.57 us -> 3.81 us
where the time goes in v6:
time: 57.9 us; the launch traced here: 57.7 us
  Pallas kernels  53.9 us (93%)
  local copies, waits for them, and re-layouts  3.81 us (7%)
    pallas_call x1, Pallas kernels, grid_body(): pl.pallas_call(functools.partial(kernel, n_z), out_shape=jax.ShapeDtypeSt...  53.9 us
    unnamed x5, local copies, waits for them, and re-layouts  3.81 us

profile of v6, /device:TPU:3, one launch (start us, length us, event | category | flops | bytes accessed | tf_op | source)
XLA Modules:
  0.0 57.7 jit_solution(9166655436251010915)
XLA Ops:
  0.0 0.0 copy-start
  0.0 1.0 %copy-done = bf16[2,8,48,256]{3,2,1,0:T(8,128)(2,1)S(1)} copy-done((bf16[2,8,48,256]{3,2,1,0:T(8,128)(2,1)S(1)}, bf16[2,8,48,256]{3,2,1,0:T(8,128)(2,1)}, u32[]{:S(2)}) %copy-start) | copy-done | bytes 393240
  1.0 0.0 copy-start.1
  1.0 0.8 %copy-done.1 = s32[48,256]{1,0:T(8,128)S(1)} copy-done((s32[48,256]{1,0:T(8,128)S(1)}, s32[48,256]{1,0:T(8,128)}, u32[]{:S(2)}) %copy-start.1) | copy-done | bytes 49176
  1.8 53.9 %shard_map.28 = bf16[2,8,512,256]{3,2,1,0:T(8,128)(2,1)S(1)} custom-call(bf16[2,8,48,256]{3,2,1,0:T(8,128)(2,1)S(1)} %copy-done, s32[48,256]{1,0:T(8,128)S(1)} %copy-done.1), custom_call_target="tpu_custom_call" | custom-call | flops 1610612736 | bytes 15728640 | tf_op jit(solution)/shard_map/pallas_call | solution.py:382
  55.7 2.0 %copy.4 = bf16[2,8,512,256]{3,2,1,0:T(8,128)(2,1)} copy(bf16[2,8,512,256]{3,2,1,0:T(8,128)(2,1)S(1)} %shard_map.28) | data formatting | bytes 8388608
Async XLA Ops:
  0.0 1.0 %copy-start = (bf16[2,8,48,256]{3,2,1,0:T(8,128)(2,1)S(1)}, bf16[2,8,48,256]{3,2,1,0:T(8,128)(2,1)}, u32[]{:S(2)}) copy-start(bf16[2,8,48,256]{3,2,1,0:T(8,128)(2,1)} %spectra_ref.1) | copy-start | bytes 1179652
  1.0 0.8 %copy-start.1 = (s32[48,256]{1,0:T(8,128)S(1)}, s32[48,256]{1,0:T(8,128)}, u32[]{:S(2)}) copy-start(s32[48,256]{1,0:T(8,128)} %alive_ref.1) | copy-start | bytes 147460
